TPU v7x, 512 devices: a whole 4x4x16 slice. The times are simulated.
512 devices in a mesh: rcv: 128 (over y, x, z_lo), frq: 4 (over z_hi, core).
Axes of the slice: x: 4, y: 4, z: 16 (z_hi: 2, z_lo: 8; z = z_hi * 8 + z_lo), core: 2. Of those that a mesh axis runs over, the one named last changes fastest.
Arguments:
- traces: bfloat16 [32, 2048, 2048], P(None, 'rcv', 'frq'), may hold values from -6 to 6
- taper_start: int32 [2048], P('rcv'), may hold values from 0 to 1023
- taper_stop: int32 [2048], P('rcv'), may hold values from 1024 to 2048
- freq_index: int32 [16], replicated, may hold values from 1472 to 1535, as said below
- kernel: bfloat16 [2, 16, 2048, 2048], P(None, 'frq', 'rcv'), may hold values from -0.5 to 0.5
Outputs:
- output_traces: float32 [32, 2048, 2048], P(None, 'rcv', 'frq')
Inputs may be any that keep to these rules, and one draw needn't show every extreme that they name: `freq_index`: distinct and increasing; the first is always the smallest allowed bin and the last always the largest.
All inputs are finite; a program needn't handle non-finite values.
Results may differ from a plain program's by a relative error of at most 0.0052.
Values may be sent and summed in bfloat16 or wider, within the bound.
A program may use at most 64 MiB of HBM per device.

v0:
```python
import math

import jax
import jax.numpy as jnp
from jax import lax
from jax.sharding import PartitionSpec as P

SOURCE_COUNT = 2048
BAND_FREQUENCIES = 16
PADDED_LENGTH = 3072


def phase_tables(freq_bins, sample_times):
    product = freq_bins[:, None] * sample_times[None, :] % PADDED_LENGTH
    phase = product.astype(jnp.float32) * (2.0 * math.pi / PADDED_LENGTH)
    return (jnp.cos(phase).astype(jnp.bfloat16), (-jnp.sin(phase)).astype(jnp.bfloat16))


def stack_spectra(trace_spectra):
    real_part = trace_spectra[:, 0]
    imag_part = trace_spectra[:, 1]
    return jnp.concatenate(
        [
            jnp.concatenate([real_part, imag_part], axis=2),
            jnp.concatenate([imag_part, -real_part], axis=2),
        ],
        axis=1,
    )


def per_device(traces, taper_start, taper_stop, freq_index, kernel):
    rows_here = traces.shape[0]
    rcv_here = traces.shape[1]
    time_here = traces.shape[2]
    sample_times = lax.axis_index("frq") * time_here + jnp.arange(time_here, dtype=jnp.int32)
    window = (sample_times[None, :] >= taper_start[:, None]) & (
        sample_times[None, :] < taper_stop[:, None]
    )
    tapered_traces = (traces * window.astype(jnp.bfloat16)[None, :, :]).reshape(
        rows_here * rcv_here, time_here
    )
    chosen = freq_index
    cosine, sine = phase_tables(chosen, sample_times)
    forward_spectra = jnp.concatenate([cosine, sine], axis=0).T
    partial_sums = jnp.dot(tapered_traces, forward_spectra, preferred_element_type=jnp.float32)
    partial_sums = partial_sums * (1.0 / math.sqrt(PADDED_LENGTH))
    trace_spectra = lax.psum_scatter(
        partial_sums.reshape(
            rows_here, rcv_here, 2, lax.axis_size("frq") * kernel.shape[1]
        ).transpose(3, 2, 0, 1),
        "frq",
        scatter_dimension=0,
        tiled=True,
    ).astype(jnp.bfloat16)
    freq_here = trace_spectra.shape[0]
    kernel_rows = jnp.concatenate([kernel[0], kernel[1]], axis=1)
    stacked = stack_spectra(trace_spectra)
    partial_resp = jnp.einsum(
        "fvr,frs->fvs", stacked, kernel_rows, preferred_element_type=jnp.float32
    )
    summed = lax.psum_scatter(
        partial_resp.transpose(2, 0, 1).reshape(
            lax.axis_size("rcv") * (SOURCE_COUNT // lax.axis_size("rcv")), freq_here * 2 * rows_here
        ),
        "rcv",
        scatter_dimension=0,
        tiled=True,
    )
    src_here = summed.shape[0]
    kernel_response = summed.astype(jnp.bfloat16).reshape(src_here, freq_here, 2, rows_here)
    piece = lax.all_gather(kernel_response, "frq", axis=1, tiled=True)
    width = piece.shape[1]
    chosen = freq_index
    cosine, sine = phase_tables(chosen, sample_times)
    inverse = jnp.concatenate([cosine, sine], axis=0)
    arranged_rows = piece.transpose(3, 0, 2, 1).reshape(rows_here * src_here, 2 * width)
    folded = jnp.dot(arranged_rows, inverse, preferred_element_type=jnp.float32)
    return (folded * (1.0 / math.sqrt(BAND_FREQUENCIES))).reshape(rows_here, src_here, time_here)


def solution(mesh):
    in_specs = (P(None, "rcv", "frq"), P("rcv"), P("rcv"), P(), P(None, "frq", "rcv", None))
    out_specs = P(None, "rcv", "frq")
    return jax.shard_map(
        per_device, mesh=mesh, in_specs=in_specs, out_specs=out_specs, check_vma=False
    )
```

profile of v0, /device:TPU:1, one launch (start us, length us, event | category | flops | bytes accessed | tf_op | source)
XLA Modules:
  0.0 1134.5 jit_solution(12115157204133112198)
XLA Ops:
  6.5 0.0 copy-start
  6.5 0.0 reduce-scatter.3.cloned.1.call-start
  6.5 0.9 cosine_convert_fusion
  7.5 0.7 and_convert_fusion
  8.2 1.1 broadcast_multiply_fusion
  9.3 0.2 convolution_multiply_fusion.1
  9.6 0.2 reshape.78
  9.8 0.2 copy.11
  10.0 39.8 %all-reduce = bf16[16,2,32,16]{2,3,0,1:T(8,128)(2,1)S(1)} all-reduce(f32[16,2,32,16]{2,3,0,1:T(8,128)S(1)} %copy.11), channel_id=2, replica_groups=mesh['rcv'=128,'frq'=4] {'frq'}, use_global_device_ids=true, to_apply=%region_0.1.clone | all-reduce | flops 16384 | bytes 98304
  49.7 1.3 dynamic-slice
  51.7 0.0 copy-done
  51.8 0.5 fusion
  52.3 1.9 copy.12
  54.2 0.0 reduce-scatter.3.cloned.1.call-update
  54.2 951.3 %reduce-scatter.3.cloned.1.call-done = f32[16,256]{1,0:T(8,128)} async-done(((f32[2048,256]{1,0:T(8,128)}), f32[16,256]{1,0:T(8,128)}) %reduce-scatter.3.cloned.1.call-update) | async-done | bytes 16400 | tf_op jit(solution)/shard_map/reduce_scatter | solution.py:61
  1005.5 0.7 convert_element_type.30
  1006.2 0.1 reshape.80
  1006.3 119.5 %all_gather.3 = bf16[16,16,2,32]{3,2,1,0:T(2,128)(2,1)S(1)} all-gather(bf16[16,4,2,32]{3,2,1,0:T(2,128)(2,1)S(1)} %reshape.80), channel_id=1, replica_groups=mesh['rcv'=128,'frq'=4] {'frq'}, dimensions={1}, use_global_device_ids=true | all-gather | bytes 40960 | tf_op jit(solution)/shard_map/all_gather | solution.py:71
  1125.8 0.2 copy.13
  1126.0 0.3 reshape.81
  1126.4 1.3 convolution_multiply_fusion
  (5 shorter events, 0.1 us)
Async XLA Ops:
  6.5 45.2 %copy-start = (bf16[2,4,16,2048]{3,2,1,0:T(8,128)(2,1)S(1)}, bf16[2,4,16,2048]{3,2,1,0:T(8,128)(2,1)}, u32[]{:S(2)}) copy-start(bf16[2,4,16,2048]{3,2,1,0:T(8,128)(2,1)} %param.9) | copy-start | bytes 1572868
  6.5 998.9 %reduce-scatter.3.cloned.1.call-start = ((), (), s32[]{:S(2)}) async-start(), calls=%async_computation.1 | async-start | bytes 2113536 | tf_op jit(solution)/shard_map/reduce_scatter | solution.py:61
Sparse Core Ops, SparseCore 0:
  54.3 951.0 reduce-scatter.2
where the time goes:
time: 1130 us
  waiting for transfers between devices  951 us (84%)
  blocking collectives  159 us (14%)
  between operations  14.1 us (1%)
    reduce_scatter x1, waiting for transfers between devices, per_device(): lax.psum_scatter(partial_resp.transpose(2, 0, 1).reshape(lax.axis_size('r...  951 us
    all_gather x1, blocking collectives, per_device(): piece = lax.all_gather(kernel_response, 'frq', axis=1, tiled=True)  120 us
    unnamed x1, blocking collectives  39.8 us
  transfers between devices with their start and end apart: 1, of which 1 were waited for; matrix products, arithmetic and copies ran while one was open for 0% of the time, Pallas kernels for 0%

commit v1 on v0

v1 whole, which is shorter than its diff:
```python
import math

import jax
import jax.numpy as jnp
from jax import lax
from jax.experimental import pallas as pl
from jax.experimental.pallas import tpu as pltpu
from jax.sharding import PartitionSpec as P

BAND_FREQUENCIES = 16
PADDED_LENGTH = 3072
MESH = pl.DeviceIdType.MESH

ROWS = 32
RCV = 16
TIME = 512
FREQS = 4
PLANE = 16
LINE = 8
GROUPS = 4
FC = 2 * FREQS
LANES = FC * ROWS
SRC = 128


def iota(shape, axis):
    return lax.broadcasted_iota(jnp.int32, shape, axis)


def column(ref, count, shape):
    rows = shape[0]
    each = rows // count
    row = iota(shape, 0) // each
    out = jnp.full(shape, ref[0], jnp.int32)
    for i in range(1, count):
        out = jnp.where(row == i, ref[i], out)
    return out


def tables(freq_ref, first_sample):
    shape = (2 * BAND_FREQUENCIES, TIME)
    bins = column(freq_ref, BAND_FREQUENCIES, shape)
    steps = bins * (first_sample + iota(shape, 1)) + (iota(shape, 0) % 2) * (PADDED_LENGTH // 4)
    steps = steps.astype(jnp.float32)
    steps = steps - jnp.floor(steps * (1.0 / PADDED_LENGTH)) * PADDED_LENGTH
    steps = jnp.where(steps < 0, steps + PADDED_LENGTH, steps)
    steps = jnp.where(steps >= PADDED_LENGTH, steps - PADDED_LENGTH, steps)
    x = (jnp.abs(steps - PADDED_LENGTH // 2) - PADDED_LENGTH // 4) * (2.0 * math.pi / PADDED_LENGTH)
    y = x * x
    poly = jnp.full(shape, -1.0 / math.factorial(11), jnp.float32)
    for power in (9, 7, 5, 3, 1):
        sign = 1.0 if power % 4 == 1 else -1.0
        poly = poly * y + sign / math.factorial(power)
    return x * poly


def body(
    start_ref,
    stop_ref,
    freq_ref,
    traces_ref,
    kernel_ref,
    out_ref,
    tr_buf,
    kbuf,
    pbuf,
    fbuf,
    gbuf,
    part,
    zbuf,
    rbuf,
    texp,
    lhs,
    local_sem,
    ks_sem,
    kr_sem,
    fs_sem,
    fr_sem,
    gs_sem,
    gr_sem,
    zs_sem,
    zr_sem,
    rs_sem,
    rr_sem,
):
    rcv = lax.axis_index("rcv")
    frq = lax.axis_index("frq")
    plane = rcv // LINE
    line = rcv % LINE

    def on_plane(i):
        peer = (plane + i) % PLANE
        return peer, (peer * LINE + line, frq)

    def on_line(i):
        peer = (line + i) % LINE
        return peer, (plane * LINE + peer, frq)

    def on_frq(i):
        peer = (frq + i) % GROUPS
        return peer, (rcv, peer)

    barrier = pltpu.get_barrier_semaphore()
    for near, count in ((on_plane, PLANE), (on_line, LINE), (on_frq, GROUPS)):

        @pl.loop(1, count)
        def _(i, near=near):
            pl.semaphore_signal(barrier, inc=1, device_id=near(i)[1], device_id_type=MESH)

    traces_copy = pltpu.make_async_copy(traces_ref, tr_buf, local_sem.at[0])
    traces_copy.start()

    def columns(peer):
        return kernel_ref.at[:, :, :, pl.ds(pl.multiple_of(peer * SRC, SRC), SRC)]

    own_copy = pltpu.make_async_copy(columns(plane), kbuf.at[:, :, plane], local_sem.at[1])
    own_copy.start()

    table = tables(freq_ref, frq * TIME).astype(jnp.bfloat16)

    pl.semaphore_wait(barrier, PLANE + LINE + GROUPS - 3)

    def kernel_send(i):
        peer, device = on_plane(i)
        return pltpu.make_async_remote_copy(
            src_ref=columns(peer),
            dst_ref=kbuf.at[:, :, plane],
            send_sem=ks_sem.at[peer],
            recv_sem=kr_sem.at[plane],
            device_id=device,
            device_id_type=MESH,
        )

    def kernel_recv(i):
        peer, device = on_plane(i)
        return pltpu.make_async_remote_copy(
            src_ref=columns(peer),
            dst_ref=kbuf.at[:, :, peer],
            send_sem=ks_sem.at[peer],
            recv_sem=kr_sem.at[peer],
            device_id=device,
            device_id_type=MESH,
        )

    @pl.loop(1, PLANE)
    def _(i):
        kernel_send(i).start()

    sample = frq * TIME + iota((RCV, TIME), 1)
    start = column(start_ref, RCV, (RCV, TIME))
    stop = column(stop_ref, RCV, (RCV, TIME))
    window = jnp.where((sample >= start) & (sample < stop), 1.0, 0.0).astype(jnp.bfloat16)
    traces_copy.wait()
    tapered = (tr_buf[...] * window[None]).reshape(ROWS * RCV, TIME)
    pbuf[...] = lax.dot_general(
        table, tapered, (((1,), (1,)), ((), ())), preferred_element_type=jnp.float32
    )

    def rows_of(peer):
        return pl.ds(pl.multiple_of(peer * FC, FC), FC)

    def sums_copy(i, to):
        peer, device = on_frq(i)
        slot = frq if to else peer
        return pltpu.make_async_remote_copy(
            src_ref=pbuf.at[rows_of(peer)],
            dst_ref=fbuf.at[slot],
            send_sem=fs_sem.at[peer],
            recv_sem=fr_sem.at[slot],
            device_id=device,
            device_id_type=MESH,
        )

    for i in range(1, GROUPS):
        sums_copy(i, True).start()
    fbuf[frq] = pbuf[rows_of(frq)]

    for i in range(2 * BAND_FREQUENCIES):
        texp[i * ROWS : (i + 1) * ROWS] = jnp.broadcast_to(table[i : i + 1], (ROWS, TIME))

    for i in range(1, GROUPS):
        sums_copy(i, False).wait_recv()
    total = ((fbuf[0] + fbuf[1]) + (fbuf[2] + fbuf[3])) * (1.0 / math.sqrt(PADDED_LENGTH))
    wide = jnp.broadcast_to(total[:, None, :], (FC, ROWS, ROWS * RCV))
    own_row = iota((FC, ROWS, ROWS * RCV), 2) // RCV == iota((FC, ROWS, ROWS * RCV), 1)
    wide = jnp.where(own_row, wide, 0.0).astype(jnp.bfloat16).reshape(LANES, ROWS * RCV)
    pick = (iota((RCV, ROWS * RCV), 1) % RCV == iota((RCV, ROWS * RCV), 0)).astype(jnp.float32)
    spectra = lax.dot_general(
        pick.astype(jnp.bfloat16), wide, (((1,), (1,)), ((), ())), preferred_element_type=jnp.float32
    )
    gbuf[plane] = spectra.astype(jnp.bfloat16)

    def spectra_copy(i, to):
        peer, device = on_plane(i)
        slot = plane if to else peer
        return pltpu.make_async_remote_copy(
            src_ref=gbuf.at[plane],
            dst_ref=gbuf.at[slot],
            send_sem=gs_sem.at[peer],
            recv_sem=gr_sem.at[slot],
            device_id=device,
            device_id_type=MESH,
        )

    @pl.loop(1, PLANE)
    def _(i):
        spectra_copy(i, True).start()

    own_copy.wait()

    @pl.loop(1, PLANE)
    def _(i):
        kernel_recv(i).wait_recv()

    @pl.loop(1, PLANE)
    def _(i):
        spectra_copy(i, False).wait_recv()

    for pair in range(FREQS // 2):
        flipped = gbuf[:, :, pair * 128 : (pair + 1) * 128].reshape(PLANE * RCV, 128)
        flipped = flipped.astype(jnp.float32).T
        halves = []
        for f in range(2):
            real = flipped[f * 64 : f * 64 + 32]
            imag = flipped[f * 64 + 32 : f * 64 + 64]
            left = jnp.concatenate([real, imag], axis=0).astype(jnp.bfloat16)
            right = jnp.concatenate([imag, -real], axis=0).astype(jnp.bfloat16)
            halves.append(
                jnp.dot(
                    left,
                    kbuf[0, pair * 2 + f].reshape(PLANE * RCV, SRC),
                    preferred_element_type=jnp.float32,
                )
                + jnp.dot(
                    right,
                    kbuf[1, pair * 2 + f].reshape(PLANE * RCV, SRC),
                    preferred_element_type=jnp.float32,
                )
            )
        part[:, pair * 128 : (pair + 1) * 128] = jnp.concatenate(halves, axis=0).T

    def source_rows(peer):
        return pl.ds(pl.multiple_of(peer * RCV, RCV), RCV)

    def line_copy(i, to):
        peer, device = on_line(i)
        slot = line if to else peer
        return pltpu.make_async_remote_copy(
            src_ref=part.at[source_rows(peer)],
            dst_ref=zbuf.at[slot],
            send_sem=zs_sem.at[peer],
            recv_sem=zr_sem.at[slot],
            device_id=device,
            device_id_type=MESH,
        )

    @pl.loop(1, LINE)
    def _(i):
        line_copy(i, True).start()

    zbuf[line] = part[source_rows(line)]

    @pl.loop(1, LINE)
    def _(i):
        line_copy(i, False).wait_recv()

    response = zbuf[0]
    for i in range(1, LINE):
        response = response + zbuf[i]
    rbuf[frq] = response.astype(jnp.bfloat16)

    def response_copy(i, to):
        peer, device = on_frq(i)
        slot = frq if to else peer
        return pltpu.make_async_remote_copy(
            src_ref=rbuf.at[frq],
            dst_ref=rbuf.at[slot],
            send_sem=rs_sem.at[peer],
            recv_sem=rr_sem.at[slot],
            device_id=device,
            device_id_type=MESH,
        )

    for i in range(1, GROUPS):
        response_copy(i, True).start()
    for i in range(1, GROUPS):
        response_copy(i, False).wait_recv()

    for j in range(GROUPS):
        terms = jnp.broadcast_to(rbuf[j].astype(jnp.float32)[None], (ROWS, RCV, LANES))
        own = iota((ROWS, RCV, LANES), 2) % ROWS == iota((ROWS, RCV, LANES), 0)
        lhs[:, j * LANES : (j + 1) * LANES] = (
            jnp.where(own, terms, 0.0).astype(jnp.bfloat16).reshape(ROWS * RCV, LANES)
        )
    traces_out = jnp.dot(lhs[...], texp[...], preferred_element_type=jnp.float32)
    out_ref[...] = (traces_out * (1.0 / math.sqrt(BAND_FREQUENCIES))).reshape(ROWS, RCV, TIME)

    @pl.loop(1, PLANE)
    def _(i):
        kernel_send(i).wait_send()
        spectra_copy(i, True).wait_send()

    @pl.loop(1, LINE)
    def _(i):
        line_copy(i, True).wait_send()

    for i in range(1, GROUPS):
        sums_copy(i, True).wait_send()
        response_copy(i, True).wait_send()


def per_device(traces, taper_start, taper_stop, freq_index, kernel):
    smem = pl.BlockSpec(memory_space=pltpu.SMEM)
    anywhere = pl.BlockSpec(memory_space=pl.ANY)
    dma = pltpu.SemaphoreType.DMA
    return pl.pallas_call(
        body,
        out_shape=jax.ShapeDtypeStruct((ROWS, RCV, TIME), jnp.float32),
        in_specs=[smem, smem, smem, anywhere, anywhere],
        out_specs=pl.BlockSpec(memory_space=pltpu.VMEM),
        scratch_shapes=[
            pltpu.VMEM((ROWS, RCV, TIME), jnp.bfloat16),
            pltpu.VMEM((2, FREQS, PLANE, RCV, SRC), jnp.bfloat16),
            pltpu.VMEM((GROUPS * FC, ROWS * RCV), jnp.float32),
            pltpu.VMEM((GROUPS, FC, ROWS * RCV), jnp.float32),
            pltpu.VMEM((PLANE, RCV, LANES), jnp.bfloat16),
            pltpu.VMEM((SRC, LANES), jnp.float32),
            pltpu.VMEM((LINE, RCV, LANES), jnp.float32),
            pltpu.VMEM((GROUPS, RCV, LANES), jnp.bfloat16),
            pltpu.VMEM((GROUPS * LANES, TIME), jnp.bfloat16),
            pltpu.VMEM((ROWS * RCV, GROUPS * LANES), jnp.bfloat16),
            dma((2,)),
            dma((PLANE,)),
            dma((PLANE,)),
            dma((GROUPS,)),
            dma((GROUPS,)),
            dma((PLANE,)),
            dma((PLANE,)),
            dma((LINE,)),
            dma((LINE,)),
            dma((GROUPS,)),
            dma((GROUPS,)),
        ],
        compiler_params=pltpu.CompilerParams(
            collective_id=0, has_side_effects=True, vmem_limit_bytes=32 * 1024 * 1024
        ),
        cost_estimate=pl.CostEstimate(
            flops=2 * 40_000_000, bytes_accessed=2 * 1024 * 1024, transcendentals=0
        ),
    )(taper_start, taper_stop, freq_index, traces, kernel)


def solution(mesh):
    in_specs = (P(None, "rcv", "frq"), P("rcv"), P("rcv"), P(), P(None, "frq", "rcv", None))
    out_specs = P(None, "rcv", "frq")
    return jax.shard_map(
        per_device, mesh=mesh, in_specs=in_specs, out_specs=out_specs, check_vma=False
    )
```

time: 1130 us -> 54 us (0.05)
  waiting for transfers between devices: 951 us -> 0 us
  blocking collectives: 159 us -> 0 us
  Pallas kernels: 0 us -> 48.7 us
  between operations: 14.1 us -> 0.01 us
    reduce_scatter x1 -> x0, waiting for transfers between devices: 951 us -> none  [per_device(): lax.psum_scatter(partial_resp.transpose(2, 0, 1).reshape(lax.axis_size('r...]
    all_gather x1 -> x0, blocking collectives: 120 us -> none  [per_device(): piece = lax.all_gather(kernel_response, 'frq', axis=1, tiled=True)]
    pallas_call x0 -> x1, Pallas kernels: none -> 48.7 us  [per_device(): pl.pallas_call(body, out_shape=jax.ShapeDtypeStruct((ROWS, RCV, TIME), jn...]
    unnamed x1 -> x0, blocking collectives: 39.8 us -> none
  transfers between devices with their start and end apart: 1 -> 0, of which waited for: 1 -> 0; matrix products, arithmetic and copies ran while one was open for 0% -> 0% of each run, Pallas kernels for 0% -> 0%
where the time goes in v1:
time: 54 us; the launch traced here: 53.8 us
  Pallas kernels  48.7 us (90%)
  local copies, waits for them, and re-layouts  5.02 us (9%)
    pallas_call x1, Pallas kernels, per_device(): pl.pallas_call(body, out_shape=jax.ShapeDtypeStruct((ROWS, RCV, TIME), jn...  48.7 us
    unnamed x11, local copies, waits for them, and re-layouts  5.02 us

profile of v1, /device:TPU:1, one launch (start us, length us, event | category | flops | bytes accessed | tf_op | source)
XLA Modules:
  0.0 53.8 jit_solution(8298837564000117640)
XLA Ops:
  0.0 0.0 copy-start
  0.0 1.0 %copy-done = bf16[32,16,512]{2,1,0:T(8,128)(2,1)S(1)} copy-done((bf16[32,16,512]{2,1,0:T(8,128)(2,1)S(1)}, bf16[32,16,512]{2,1,0:T(8,128)(2,1)}, u32[]{:S(2)}) %copy-start) | copy-done | bytes 524312
  1.0 0.0 copy-start.1
  1.0 1.0 %copy-done.1 = bf16[2,4,16,2048]{3,2,1,0:T(8,128)(2,1)S(1)} copy-done((bf16[2,4,16,2048]{3,2,1,0:T(8,128)(2,1)S(1)}, bf16[2,4,16,2048]{3,2,1,0:T(8,128)(2,1)}, u32[]{:S(2)}) %copy-start.1) | copy-done | bytes 524312
  2.1 0.0 copy-start.2
  2.1 0.7 %copy-done.2 = s32[16]{0:T(128)S(1)} copy-done((s32[16]{0:T(128)S(1)}, s32[16]{0:T(128)}, u32[]{:S(2)}) %copy-start.2) | copy-done | bytes 88
  2.7 0.0 copy-start.3
  2.7 0.7 %copy-done.3 = s32[16]{0:T(128)S(1)} copy-done((s32[16]{0:T(128)S(1)}, s32[16]{0:T(128)}, u32[]{:S(2)}) %copy-start.3) | copy-done | bytes 88
  3.4 0.0 copy-start.4
  3.4 0.7 %copy-done.4 = s32[16]{0:T(128)S(1)} copy-done((s32[16]{0:T(128)S(1)}, s32[16]{0:T(128)}, u32[]{:S(2)}) %copy-start.4) | copy-done | bytes 88
  4.1 48.7 %shard_map.55 = f32[32,16,512]{2,1,0:T(8,128)S(1)} custom-call(s32[16]{0:T(128)S(1)} %copy-done.2, s32[16]{0:T(128)S(1)} %copy-done.3, s32[16]{0:T(128)S(1)} %copy-done.4, bf16[32,16,512]{2,1,0:T(8,128)(2,1)S(1)} %copy-done, bf16[2,4,16,2048]{3,2,1,0:T(8,128)(2,1)S(1)} %copy-done.1), custom_call_target="tpu_custom_call" | custom-call | flops 80000000 | bytes 2097152 | tf_op jit(solution)/shard_map/pallas_call | solution.py:316
  52.8 1.0 %copy.7 = f32[32,16,512]{2,1,0:T(8,128)} copy(f32[32,16,512]{2,1,0:T(8,128)S(1)} %shard_map.55) | data formatting | bytes 2097152
Async XLA Ops:
  0.0 1.0 %copy-start = (bf16[32,16,512]{2,1,0:T(8,128)(2,1)S(1)}, bf16[32,16,512]{2,1,0:T(8,128)(2,1)}, u32[]{:S(2)}) copy-start(bf16[32,16,512]{2,1,0:T(8,128)(2,1)} %traces_ref.1) | copy-start | bytes 1572868
  1.0 1.0 %copy-start.1 = (bf16[2,4,16,2048]{3,2,1,0:T(8,128)(2,1)S(1)}, bf16[2,4,16,2048]{3,2,1,0:T(8,128)(2,1)}, u32[]{:S(2)}) copy-start(bf16[2,4,16,2048]{3,2,1,0:T(8,128)(2,1)} %kernel_ref.1) | copy-start | bytes 1572868
  2.1 0.7 %copy-start.2 = (s32[16]{0:T(128)S(1)}, s32[16]{0:T(128)}, u32[]{:S(2)}) copy-start(s32[16]{0:T(128)} %start_ref.1) | copy-start | bytes 196
  2.7 0.7 %copy-start.3 = (s32[16]{0:T(128)S(1)}, s32[16]{0:T(128)}, u32[]{:S(2)}) copy-start(s32[16]{0:T(128)} %stop_ref.1) | copy-start | bytes 196
  3.4 0.7 %copy-start.4 = (s32[16]{0:T(128)S(1)}, s32[16]{0:T(128)}, u32[]{:S(2)}) copy-start(s32[16]{0:T(128)} %freq_ref.1) | copy-start | bytes 196

commit v2 on v1

v2 whole, which is shorter than its diff:
```python
import math

import jax
import jax.numpy as jnp
from jax import lax
from jax.experimental import pallas as pl
from jax.experimental.pallas import tpu as pltpu
from jax.sharding import PartitionSpec as P

BAND_FREQUENCIES = 16
PADDED_LENGTH = 3072
MESH = pl.DeviceIdType.MESH

ROWS = 32
RCV = 16
TIME = 512
FREQS = 4
PLANE = 16
LINE = 8
RING = 16
GROUPS = 4
FC = 2 * FREQS
LANES = FC * ROWS
SRC = 128
HALF = ROWS // 2
PLANE_STEPS = (
    (2, 2), (2, 1), (2, 3), (1, 2), (3, 2), (1, 1), (1, 3), (3, 1),
    (3, 3), (2, 0), (0, 2), (1, 0), (3, 0), (0, 1), (0, 3),
)
RING_STEPS = (8, 7, 9, 6, 10, 5, 11, 4, 12, 3, 13, 2, 14, 1, 15)


def iota(shape, axis):
    return lax.broadcasted_iota(jnp.int32, shape, axis)


def column(ref, count, shape):
    rows = shape[0]
    each = rows // count
    row = iota(shape, 0) // each
    out = jnp.full(shape, ref[0], jnp.int32)
    for i in range(1, count):
        out = jnp.where(row == i, ref[i], out)
    return out


def tables(freq_ref, first_sample):
    shape = (2 * BAND_FREQUENCIES, TIME)
    bins = column(freq_ref, BAND_FREQUENCIES, shape)
    steps = bins * (first_sample + iota(shape, 1)) + (iota(shape, 0) % 2) * (PADDED_LENGTH // 4)
    steps = steps.astype(jnp.float32)
    steps = steps - jnp.floor(steps * (1.0 / PADDED_LENGTH)) * PADDED_LENGTH
    steps = jnp.where(steps < 0, steps + PADDED_LENGTH, steps)
    steps = jnp.where(steps >= PADDED_LENGTH, steps - PADDED_LENGTH, steps)
    x = (jnp.abs(steps - PADDED_LENGTH // 2) - PADDED_LENGTH // 4) * (2.0 * math.pi / PADDED_LENGTH)
    y = x * x
    poly = jnp.full(shape, -1.0 / math.factorial(11), jnp.float32)
    for power in (9, 7, 5, 3, 1):
        sign = 1.0 if power % 4 == 1 else -1.0
        poly = poly * y + sign / math.factorial(power)
    return x * poly


def body(
    start_hbm,
    stop_hbm,
    freq_hbm,
    traces_ref,
    kernel_ref,
    response_ref,
    table_ref,
    start_ref,
    stop_ref,
    freq_ref,
    tr_buf,
    kbuf,
    pown,
    pbuf,
    fbuf,
    gbuf,
    part,
    pout,
    zbuf,
    rbuf,
    local_sem,
    ks_sem,
    kr_sem,
    fs_sem,
    fr_sem,
    gs_sem,
    gr_sem,
    zs_sem,
    zr_sem,
    rs_sem,
    rr_sem,
):
    rcv = lax.axis_index("rcv")
    frq = lax.axis_index("frq")
    plane = rcv // LINE
    line = rcv % LINE
    high = frq // 2
    core = frq % 2
    ring = high * LINE + line
    row = plane // 4
    col = plane % 4

    on_plane = []
    for across, down in PLANE_STEPS:
        peer = ((row + down) % 4) * 4 + (col + across) % 4
        on_plane.append((peer, (peer * LINE + line, frq)))
    on_ring = []
    for step in RING_STEPS:
        peer = (ring + step) % RING
        on_ring.append((peer, (plane * LINE + peer % LINE, (peer // LINE) * 2 + core)))
    sibling = (rcv, high * 2 + 1 - core)
    on_frq = [
        (peer, (rcv, peer))
        for peer in ((1 - high) * 2 + 1 - core, (1 - high) * 2 + core, high * 2 + 1 - core)
    ]

    barrier = pltpu.get_barrier_semaphore()
    greeted = on_ring + on_frq[:1] + on_frq[2:] + on_plane
    for _, device in greeted:
        pl.semaphore_signal(barrier, inc=1, device_id=device, device_id_type=MESH)

    traces_copy = pltpu.make_async_copy(traces_ref, tr_buf, local_sem.at[0])
    traces_copy.start()
    index_copies = [
        pltpu.make_async_copy(source, target, local_sem.at[2 + i])
        for i, (source, target) in enumerate(
            ((freq_hbm, freq_ref), (start_hbm, start_ref), (stop_hbm, stop_ref))
        )
    ]
    for copy in index_copies:
        copy.start()

    def columns(peer):
        return kernel_ref.at[:, :, :, pl.ds(pl.multiple_of(peer * SRC, SRC), SRC)]

    own_copy = pltpu.make_async_copy(columns(plane), kbuf.at[:, :, plane], local_sem.at[1])
    own_copy.start()

    for copy in index_copies:
        copy.wait()
    table = tables(freq_ref, frq * TIME).astype(jnp.bfloat16)

    sample = frq * TIME + iota((RCV, TIME), 1)
    start = column(start_ref, RCV, (RCV, TIME))
    stop = column(stop_ref, RCV, (RCV, TIME))
    window = jnp.where((sample >= start) & (sample < stop), 1.0, 0.0).astype(jnp.bfloat16)
    traces_copy.wait()
    tapered = (tr_buf[...] * window[None]).reshape(ROWS * RCV, TIME)
    sums = lax.dot_general(
        table, tapered, (((1,), (1,)), ((), ())), preferred_element_type=jnp.float32
    )
    for j in range(GROUPS):
        for half in range(2):
            piece = sums[j * FC : (j + 1) * FC, half * 256 : (half + 1) * 256]
            pown[j, half * FC : (half + 1) * FC] = piece
    pbuf[...] = pown[...].astype(jnp.bfloat16)

    pl.semaphore_wait(barrier, len(greeted))

    def sums_copy(to, slot, device):
        return pltpu.make_async_remote_copy(
            src_ref=pbuf.at[to],
            dst_ref=fbuf.at[slot],
            send_sem=fs_sem.at[to],
            recv_sem=fr_sem.at[slot],
            device_id=device,
            device_id_type=MESH,
        )

    for peer, device in on_frq:
        sums_copy(peer, frq, device).start()

    def kernel_copy(to, slot, device):
        return pltpu.make_async_remote_copy(
            src_ref=columns(to),
            dst_ref=kbuf.at[:, :, slot],
            send_sem=ks_sem.at[to],
            recv_sem=kr_sem.at[slot],
            device_id=device,
            device_id_type=MESH,
        )

    for peer, device in on_plane:
        kernel_copy(peer, plane, device).start()

    table_ref[...] = table

    total = pown[frq]
    for peer, device in on_frq:
        sums_copy(peer, peer, device).wait_recv()
    for peer, device in on_frq:
        total = total + fbuf[peer].astype(jnp.float32)
    total = total * (1.0 / math.sqrt(PADDED_LENGTH))
    spread = (FC, HALF, HALF * RCV)
    own_row = iota(spread, 2) // RCV == iota(spread, 1)
    pick = iota((RCV, HALF * RCV), 1) % RCV == iota((RCV, HALF * RCV), 0)
    pick = jnp.where(pick, 1.0, 0.0).astype(jnp.bfloat16)
    for half in range(2):
        wide = jnp.broadcast_to(total[half * FC : (half + 1) * FC][:, None, :], spread)
        wide = jnp.where(own_row, wide, 0.0).astype(jnp.bfloat16).reshape(FC * HALF, HALF * RCV)
        spectra = lax.dot_general(
            pick, wide, (((1,), (1,)), ((), ())), preferred_element_type=jnp.float32
        )
        gbuf[plane, :, half * 128 : (half + 1) * 128] = spectra.astype(jnp.bfloat16)

    def spectra_copy(to, slot, device):
        return pltpu.make_async_remote_copy(
            src_ref=gbuf.at[plane],
            dst_ref=gbuf.at[slot],
            send_sem=gs_sem.at[to],
            recv_sem=gr_sem.at[slot],
            device_id=device,
            device_id_type=MESH,
        )

    for peer, device in on_plane:
        spectra_copy(peer, plane, device).start()

    own_copy.wait()
    for peer, device in on_plane:
        kernel_copy(peer, peer, device).wait_recv()
    for peer, device in on_plane:
        spectra_copy(peer, peer, device).wait_recv()

    flipped = []
    for half in range(2):
        block = gbuf[:, :, half * 128 : (half + 1) * 128].reshape(PLANE * RCV, 128)
        flipped.append(block.astype(jnp.float32).T)
    for pair in range(FREQS // 2):
        halves = []
        for f in (pair * 2, pair * 2 + 1):
            at = f * 2 * HALF
            real = [block[at : at + HALF] for block in flipped]
            imag = [block[at + HALF : at + 2 * HALF] for block in flipped]
            left = jnp.concatenate(real + imag, axis=0).astype(jnp.bfloat16)
            right = jnp.concatenate(imag + [-block for block in real], axis=0).astype(jnp.bfloat16)
            halves.append(
                jnp.dot(
                    left, kbuf[0, f].reshape(PLANE * RCV, SRC), preferred_element_type=jnp.float32
                )
                + jnp.dot(
                    right, kbuf[1, f].reshape(PLANE * RCV, SRC), preferred_element_type=jnp.float32
                )
            )
        turned = jnp.concatenate(halves, axis=0).T
        part[:, pair * 128 : (pair + 1) * 128] = turned
        pout[:, pair * 128 : (pair + 1) * 128] = turned.astype(jnp.bfloat16)

    def source_rows(place):
        return pl.ds(pl.multiple_of((place % LINE) * RCV, RCV), RCV)

    def ring_copy(to, slot, device):
        return pltpu.make_async_remote_copy(
            src_ref=pout.at[source_rows(to)],
            dst_ref=zbuf.at[slot],
            send_sem=zs_sem.at[to],
            recv_sem=zr_sem.at[slot],
            device_id=device,
            device_id_type=MESH,
        )

    for peer, device in on_ring:
        ring_copy(peer, ring, device).start()

    zbuf[ring] = jnp.zeros((RCV, LANES), jnp.bfloat16)
    near = part[source_rows(ring)]
    far = jnp.zeros((RCV, LANES), jnp.float32)

    for peer, device in on_ring:
        ring_copy(peer, peer, device).wait_recv()

    for i in range(LINE):
        near = near + zbuf[high * LINE + i].astype(jnp.float32)
        far = far + zbuf[(1 - high) * LINE + i].astype(jnp.float32)
    rbuf[core, high] = near.astype(jnp.bfloat16)
    rbuf[core, 1 - high] = far.astype(jnp.bfloat16)

    def response_copy(slot):
        return pltpu.make_async_remote_copy(
            src_ref=rbuf.at[core],
            dst_ref=rbuf.at[slot],
            send_sem=rs_sem,
            recv_sem=rr_sem,
            device_id=sibling,
            device_id_type=MESH,
        )

    response_copy(core).start()
    response_copy(1 - core).wait_recv()
    for j in range(GROUPS):
        response_ref[j] = rbuf[j % 2, j // 2]

    for peer, device in on_plane:
        kernel_copy(peer, plane, device).wait_send()
        spectra_copy(peer, plane, device).wait_send()
    for peer, device in on_frq:
        sums_copy(peer, frq, device).wait_send()
    for peer, device in on_ring:
        ring_copy(peer, ring, device).wait_send()
    response_copy(core).wait_send()


def inverse(response_ref, table_ref, out_ref, texp, lhs):
    for i in range(2 * BAND_FREQUENCIES):
        texp[i * ROWS : (i + 1) * ROWS] = jnp.broadcast_to(table_ref[i : i + 1], (ROWS, TIME))
    for j in range(GROUPS):
        terms = jnp.broadcast_to(response_ref[j].astype(jnp.float32)[None], (ROWS, RCV, LANES))
        own = iota((ROWS, RCV, LANES), 2) % ROWS == iota((ROWS, RCV, LANES), 0)
        lhs[:, j * LANES : (j + 1) * LANES] = (
            jnp.where(own, terms, 0.0).astype(jnp.bfloat16).reshape(ROWS * RCV, LANES)
        )
    traces_out = jnp.dot(lhs[...], texp[...], preferred_element_type=jnp.float32)
    out_ref[...] = (traces_out * (1.0 / math.sqrt(BAND_FREQUENCIES))).reshape(ROWS, RCV, TIME)


def per_device(traces, taper_start, taper_stop, freq_index, kernel):
    vmem = pl.BlockSpec(memory_space=pltpu.VMEM)
    hbm = pl.BlockSpec(memory_space=pltpu.HBM)
    dma = pltpu.SemaphoreType.DMA
    response, table = pl.pallas_call(
        body,
        out_shape=[
            jax.ShapeDtypeStruct((GROUPS, RCV, LANES), jnp.bfloat16),
            jax.ShapeDtypeStruct((2 * BAND_FREQUENCIES, TIME), jnp.bfloat16),
        ],
        in_specs=[hbm] * 5,
        out_specs=[vmem] * 2,
        scratch_shapes=[
            pltpu.SMEM((RCV,), jnp.int32),
            pltpu.SMEM((RCV,), jnp.int32),
            pltpu.SMEM((BAND_FREQUENCIES,), jnp.int32),
            pltpu.VMEM((ROWS, RCV, TIME), jnp.bfloat16),
            pltpu.VMEM((2, FREQS, PLANE, RCV, SRC), jnp.bfloat16),
            pltpu.VMEM((GROUPS, 2 * FC, HALF * RCV), jnp.float32),
            pltpu.VMEM((GROUPS, 2 * FC, HALF * RCV), jnp.bfloat16),
            pltpu.VMEM((GROUPS, 2 * FC, HALF * RCV), jnp.bfloat16),
            pltpu.VMEM((PLANE, RCV, LANES), jnp.bfloat16),
            pltpu.VMEM((SRC, LANES), jnp.float32),
            pltpu.VMEM((SRC, LANES), jnp.bfloat16),
            pltpu.VMEM((RING, RCV, LANES), jnp.bfloat16),
            pltpu.VMEM((2, 2, RCV, LANES), jnp.bfloat16),
            dma((5,)),
            dma((PLANE,)),
            dma((PLANE,)),
            dma((GROUPS,)),
            dma((GROUPS,)),
            dma((PLANE,)),
            dma((PLANE,)),
            dma((RING,)),
            dma((RING,)),
            dma,
            dma,
        ],
        compiler_params=pltpu.CompilerParams(
            collective_id=0, has_side_effects=True, vmem_limit_bytes=60 * 1024 * 1024
        ),
        cost_estimate=pl.CostEstimate(
            flops=2 * 40_000_000, bytes_accessed=1024 * 1024, transcendentals=0
        ),
    )(taper_start, taper_stop, freq_index, traces, kernel)
    return pl.pallas_call(
        inverse,
        out_shape=jax.ShapeDtypeStruct((ROWS, RCV, TIME), jnp.float32),
        in_specs=[vmem] * 2,
        out_specs=vmem,
        scratch_shapes=[
            pltpu.VMEM((GROUPS * LANES, TIME), jnp.bfloat16),
            pltpu.VMEM((ROWS * RCV, GROUPS * LANES), jnp.bfloat16),
        ],
        compiler_params=pltpu.CompilerParams(vmem_limit_bytes=60 * 1024 * 1024),
        cost_estimate=pl.CostEstimate(
            flops=2 * 8_400_000, bytes_accessed=1024 * 1024, transcendentals=0
        ),
    )(response, table)


def solution(mesh):
    in_specs = (P(None, "rcv", "frq"), P("rcv"), P("rcv"), P(), P(None, "frq", "rcv", None))
    out_specs = P(None, "rcv", "frq")
    return jax.shard_map(
        per_device, mesh=mesh, in_specs=in_specs, out_specs=out_specs, check_vma=False
    )
```

time: 54 us -> 44.2 us (0.82)
  local copies, waits for them, and re-layouts: 5.02 us -> 0 us
  Pallas kernels: 48.7 us -> 44 us
    unnamed x11 -> x0, local copies, waits for them, and re-layouts: 5.02 us -> none
    pallas_call x1 -> x2, Pallas kernels: 48.7 us -> 44 us  [the longest x1 41.6 us: per_device(): pl.pallas_call(body, out_shape=[jax.ShapeDtypeStruct((GROUPS, RCV, LANES)...]
where the time goes in v2:
time: 44.2 us; the launch traced here: 44 us
  Pallas kernels  44 us (100%)
    pallas_call x1, Pallas kernels, per_device(): pl.pallas_call(body, out_shape=[jax.ShapeDtypeStruct((GROUPS, RCV, LANES)...  41.6 us
    pallas_call x1, Pallas kernels, per_device(): pl.pallas_call(inverse, out_shape=jax.ShapeDtypeStruct((ROWS, RCV, TIME),...  2.46 us

profile of v2, /device:TPU:1, one launch (start us, length us, event | category | flops | bytes accessed | tf_op | source)
XLA Modules:
  0.0 44.0 jit_solution(5599500313503200684)
XLA Ops:
  0.0 41.6 %shard_map.55 = (bf16[4,16,256]{2,1,0:T(8,128)(2,1)}, bf16[32,512]{1,0:T(8,128)(2,1)}) custom-call(s32[16]{0:T(128)} %start_hbm.1, s32[16]{0:T(128)} %stop_hbm.1, s32[16]{0:T(128)} %freq_hbm.1, bf16[32,16,512]{2,1,0:T(8,128)(2,1)} %traces_ref.1, bf16[2,4,16,2048]{3,2,1,0:T(8,128)(2,1)} %kernel_ref.1), custom_call_target="tpu_custom_call" | custom-call | flops 80000000 | bytes 1048576 | tf_op jit(solution)/shard_map/pallas_call | solution.py:324
  41.6 2.5 %shard_map.56 = f32[32,16,512]{2,1,0:T(8,128)} custom-call(bf16[4,16,256]{2,1,0:T(8,128)(2,1)} %get-tuple-element.7.response_ref, bf16[32,512]{1,0:T(8,128)(2,1)} %get-tuple-element.8.table_ref), custom_call_target="tpu_custom_call" | custom-call | flops 16800000 | bytes 1048576 | tf_op jit(solution)/shard_map/pallas_call | solution.py:365

commit v3 on v2

--- a/solution.py
+++ b/solution.py
@@ -23,11 +23,11 @@
 LANES = FC * ROWS
 SRC = 128
 HALF = ROWS // 2
+PIECE = 256
 PLANE_STEPS = (
     (2, 2), (2, 1), (2, 3), (1, 2), (3, 2), (1, 1), (1, 3), (3, 1),
     (3, 3), (2, 0), (0, 2), (1, 0), (3, 0), (0, 1), (0, 3),
 )
-RING_STEPS = (8, 7, 9, 6, 10, 5, 11, 4, 12, 3, 13, 2, 14, 1, 15)
 
 
 def iota(shape, axis):
@@ -82,6 +82,7 @@
     pout,
     zbuf,
     rbuf,
+    table_buf,
     local_sem,
     ks_sem,
     kr_sem,
@@ -109,8 +110,8 @@
         peer = ((row + down) % 4) * 4 + (col + across) % 4
         on_plane.append((peer, (peer * LINE + line, frq)))
     on_ring = []
-    for step in RING_STEPS:
-        peer = (ring + step) % RING
+    for i in range(RING - 1):
+        peer = i + (i + RING - ring) // RING
         on_ring.append((peer, (plane * LINE + peer % LINE, (peer // LINE) * 2 + core)))
     sibling = (rcv, high * 2 + 1 - core)
     on_frq = [
@@ -119,7 +120,7 @@
     ]
 
     barrier = pltpu.get_barrier_semaphore()
-    greeted = on_ring + on_frq[:1] + on_frq[2:] + on_plane
+    greeted = on_frq[:1] + on_ring + on_plane + on_frq[2:]
     for _, device in greeted:
         pl.semaphore_signal(barrier, inc=1, device_id=device, device_id_type=MESH)
 
@@ -187,7 +188,9 @@
     for peer, device in on_plane:
         kernel_copy(peer, plane, device).start()
 
-    table_ref[...] = table
+    table_buf[...] = table
+    table_copy = pltpu.make_async_copy(table_buf, table_ref, local_sem.at[5])
+    table_copy.start()
 
     total = pown[frq]
     for peer, device in on_frq:
@@ -276,13 +279,13 @@
     for i in range(LINE):
         near = near + zbuf[high * LINE + i].astype(jnp.float32)
         far = far + zbuf[(1 - high) * LINE + i].astype(jnp.float32)
-    rbuf[core, high] = near.astype(jnp.bfloat16)
-    rbuf[core, 1 - high] = far.astype(jnp.bfloat16)
+    rbuf[high] = near.astype(jnp.bfloat16)
+    rbuf[1 - high] = far.astype(jnp.bfloat16)
 
     def response_copy(slot):
         return pltpu.make_async_remote_copy(
-            src_ref=rbuf.at[core],
-            dst_ref=rbuf.at[slot],
+            src_ref=rbuf,
+            dst_ref=response_ref.at[slot],
             send_sem=rs_sem,
             recv_sem=rr_sem,
             device_id=sibling,
@@ -290,9 +293,8 @@
         )
 
     response_copy(core).start()
-    response_copy(1 - core).wait_recv()
-    for j in range(GROUPS):
-        response_ref[j] = rbuf[j % 2, j // 2]
+    own_response = pltpu.make_async_copy(rbuf, response_ref.at[core], local_sem.at[6])
+    own_response.start()
 
     for peer, device in on_plane:
         kernel_copy(peer, plane, device).wait_send()
@@ -301,34 +303,70 @@
         sums_copy(peer, frq, device).wait_send()
     for peer, device in on_ring:
         ring_copy(peer, ring, device).wait_send()
+
+    table_copy.wait()
+    own_response.wait()
     response_copy(core).wait_send()
-
-
-def inverse(response_ref, table_ref, out_ref, texp, lhs):
-    for i in range(2 * BAND_FREQUENCIES):
-        texp[i * ROWS : (i + 1) * ROWS] = jnp.broadcast_to(table_ref[i : i + 1], (ROWS, TIME))
-    for j in range(GROUPS):
-        terms = jnp.broadcast_to(response_ref[j].astype(jnp.float32)[None], (ROWS, RCV, LANES))
-        own = iota((ROWS, RCV, LANES), 2) % ROWS == iota((ROWS, RCV, LANES), 0)
-        lhs[:, j * LANES : (j + 1) * LANES] = (
-            jnp.where(own, terms, 0.0).astype(jnp.bfloat16).reshape(ROWS * RCV, LANES)
-        )
-    traces_out = jnp.dot(lhs[...], texp[...], preferred_element_type=jnp.float32)
-    out_ref[...] = (traces_out * (1.0 / math.sqrt(BAND_FREQUENCIES))).reshape(ROWS, RCV, TIME)
+    response_copy(1 - core).wait_recv()
+
+
+def inverse(response_hbm, table_hbm, out_hbm, response, table, texp, lhs, result, in_sem, out_sem):
+    copies = [
+        pltpu.make_async_copy(table_hbm, table, in_sem.at[0]),
+        pltpu.make_async_copy(response_hbm, response, in_sem.at[1]),
+    ]
+    for copy in copies:
+        copy.start()
+    own = iota((8, RCV, 128), 2) % 8 == iota((8, RCV, 128), 0)
+    own = jnp.where(own, 1.0, 0.0).astype(jnp.bfloat16)
+    slot = iota((RCV, 128), 1) // 8 % 4
+    copies[0].wait()
+    for m in range(2):
+        for q in range(4):
+            for i in range(4):
+                row = (4 * m + i) * 4 + q
+                at = m * 128 + 32 * q + 8 * i
+                texp[at : at + 8] = jnp.broadcast_to(table[row : row + 1], (8, TIME))
+    copies[1].wait()
+    for m in range(2):
+        tiles = []
+        for i in range(4):
+            j, half = (4 * m + i) // 2, i % 2
+            tile = response[j % 2, j // 2, :, half * 128 : (half + 1) * 128]
+            tiles.append(tile.astype(jnp.float32))
+        for a in range(ROWS // 8):
+            merged = tiles[a]
+            for i in range(4):
+                if i != a:
+                    turned = pltpu.roll(tiles[i], 8 * (i - a) % 128, 1)
+                    merged = jnp.where(slot == i, turned, merged)
+            terms = merged.astype(jnp.bfloat16)[None] * own
+            lhs[a * 128 : (a + 1) * 128, m * 128 : (m + 1) * 128] = terms.reshape(128, 128)
+    pieces = []
+    for n in range(TIME // PIECE):
+        samples = slice(n * PIECE, (n + 1) * PIECE)
+        traces_out = jnp.dot(lhs[...], texp[:, samples], preferred_element_type=jnp.float32)
+        traces_out = traces_out * (1.0 / math.sqrt(BAND_FREQUENCIES))
+        result[n] = traces_out.reshape(ROWS, RCV, PIECE)
+        pieces.append(
+            pltpu.make_async_copy(result.at[n], out_hbm.at[:, :, samples], out_sem.at[n])
+        )
+        pieces[-1].start()
+    for piece in pieces:
+        piece.wait()
 
 
 def per_device(traces, taper_start, taper_stop, freq_index, kernel):
-    vmem = pl.BlockSpec(memory_space=pltpu.VMEM)
     hbm = pl.BlockSpec(memory_space=pltpu.HBM)
     dma = pltpu.SemaphoreType.DMA
     response, table = pl.pallas_call(
         body,
         out_shape=[
-            jax.ShapeDtypeStruct((GROUPS, RCV, LANES), jnp.bfloat16),
+            jax.ShapeDtypeStruct((2, 2, RCV, LANES), jnp.bfloat16),
             jax.ShapeDtypeStruct((2 * BAND_FREQUENCIES, TIME), jnp.bfloat16),
         ],
         in_specs=[hbm] * 5,
-        out_specs=[vmem] * 2,
+        out_specs=[hbm] * 2,
         scratch_shapes=[
             pltpu.SMEM((RCV,), jnp.int32),
             pltpu.SMEM((RCV,), jnp.int32),
@@ -342,8 +380,9 @@
             pltpu.VMEM((SRC, LANES), jnp.float32),
             pltpu.VMEM((SRC, LANES), jnp.bfloat16),
             pltpu.VMEM((RING, RCV, LANES), jnp.bfloat16),
-            pltpu.VMEM((2, 2, RCV, LANES), jnp.bfloat16),
-            dma((5,)),
+            pltpu.VMEM((2, RCV, LANES), jnp.bfloat16),
+            pltpu.VMEM((2 * BAND_FREQUENCIES, TIME), jnp.bfloat16),
+            dma((7,)),
             dma((PLANE,)),
             dma((PLANE,)),
             dma((GROUPS,)),
@@ -365,11 +404,16 @@
     return pl.pallas_call(
         inverse,
         out_shape=jax.ShapeDtypeStruct((ROWS, RCV, TIME), jnp.float32),
-        in_specs=[vmem] * 2,
-        out_specs=vmem,
+        in_specs=[hbm] * 2,
+        out_specs=hbm,
         scratch_shapes=[
-            pltpu.VMEM((GROUPS * LANES, TIME), jnp.bfloat16),
-            pltpu.VMEM((ROWS * RCV, GROUPS * LANES), jnp.bfloat16),
+            pltpu.VMEM((2, 2, RCV, LANES), jnp.bfloat16),
+            pltpu.VMEM((2 * BAND_FREQUENCIES, TIME), jnp.bfloat16),
+            pltpu.VMEM((256, TIME), jnp.bfloat16),
+            pltpu.VMEM((ROWS * RCV, 256), jnp.bfloat16),
+            pltpu.VMEM((TIME // PIECE, ROWS, RCV, PIECE), jnp.float32),
+            dma((2,)),
+            dma((TIME // PIECE,)),
         ],
         compiler_params=pltpu.CompilerParams(vmem_limit_bytes=60 * 1024 * 1024),
         cost_estimate=pl.CostEstimate(

time: 44.2 us -> 43.3 us (0.980)
  Pallas kernels: 44 us -> 43 us
    pallas_call x1, Pallas kernels: 41.6 us -> 40.9 us  [per_device(): pl.pallas_call(body, out_shape=[jax.ShapeDtypeStruct((2, 2, RCV, LANES),...]
where the time goes in v3:
time: 43.3 us; the launch traced here: 43.1 us
  Pallas kernels  43 us (99%)
    pallas_call x1, Pallas kernels, per_device(): pl.pallas_call(body, out_shape=[jax.ShapeDtypeStruct((2, 2, RCV, LANES),...  40.9 us
    pallas_call x1, Pallas kernels, per_device(): pl.pallas_call(inverse, out_shape=jax.ShapeDtypeStruct((ROWS, RCV, TIME),...  2.16 us

profile of v3, /device:TPU:1, one launch (start us, length us, event | category | flops | bytes accessed | tf_op | source)
XLA Modules:
  0.0 43.1 jit_solution(16375655697387133604)
XLA Ops:
  0.0 40.9 %shard_map.55 = (bf16[2,2,16,256]{3,2,1,0:T(8,128)(2,1)}, bf16[32,512]{1,0:T(8,128)(2,1)}) custom-call(s32[16]{0:T(128)} %start_hbm.1, s32[16]{0:T(128)} %stop_hbm.1, s32[16]{0:T(128)} %freq_hbm.1, bf16[32,16,512]{2,1,0:T(8,128)(2,1)} %traces_ref.1, bf16[2,4,16,2048]{3,2,1,0:T(8,128)(2,1)} %kernel_ref.1), custom_call_target="tpu_custom_call" | custom-call | flops 80000000 | bytes 1048576 | tf_op jit(solution)/shard_map/pallas_call | solution.py:362
  40.9 2.2 %shard_map.56 = f32[32,16,512]{2,1,0:T(8,128)} custom-call(bf16[2,2,16,256]{3,2,1,0:T(8,128)(2,1)} %get-tuple-element.7.response_hbm, bf16[32,512]{1,0:T(8,128)(2,1)} %get-tuple-element.8.table_hbm), custom_call_target="tpu_custom_call" | custom-call | flops 16800000 | bytes 1048576 | tf_op jit(solution)/shard_map/pallas_call | solution.py:404

commit v4 on v3

v4 whole, which is shorter than its diff:
```python
import math

import jax
import jax.numpy as jnp
from jax import lax
from jax.experimental import pallas as pl
from jax.experimental.pallas import tpu as pltpu
from jax.sharding import PartitionSpec as P

BAND_FREQUENCIES = 16
PADDED_LENGTH = 3072
MESH = pl.DeviceIdType.MESH

ROWS = 32
RCV = 16
TIME = 512
FREQS = 4
PLANE = 16
LINE = 8
RING = 16
GROUPS = 4
FC = 2 * FREQS
LANES = FC * ROWS
SRC = 128
HALF = ROWS // 2
PIECE = 256
PLANE_STEPS = (
    (2, 2), (2, 1), (2, 3), (1, 2), (3, 2), (1, 1), (1, 3), (3, 1),
    (3, 3), (2, 0), (0, 2), (1, 0), (3, 0), (0, 1), (0, 3),
)


def iota(shape, axis):
    return lax.broadcasted_iota(jnp.int32, shape, axis)


def column(ref, count, shape):
    rows = shape[0]
    each = rows // count
    row = iota(shape, 0) // each
    out = jnp.full(shape, ref[0], jnp.int32)
    for i in range(1, count):
        out = jnp.where(row == i, ref[i], out)
    return out


def tables(freq_ref, first_sample):
    shape = (2 * BAND_FREQUENCIES, TIME)
    bins = column(freq_ref, BAND_FREQUENCIES, shape)
    steps = bins * (first_sample + iota(shape, 1)) + (iota(shape, 0) % 2) * (PADDED_LENGTH // 4)
    steps = steps.astype(jnp.float32)
    steps = steps - jnp.floor(steps * (1.0 / PADDED_LENGTH)) * PADDED_LENGTH
    steps = jnp.where(steps < 0, steps + PADDED_LENGTH, steps)
    steps = jnp.where(steps >= PADDED_LENGTH, steps - PADDED_LENGTH, steps)
    x = (jnp.abs(steps - PADDED_LENGTH // 2) - PADDED_LENGTH // 4) * (2.0 * math.pi / PADDED_LENGTH)
    y = x * x
    poly = jnp.full(shape, -1.0 / math.factorial(11), jnp.float32)
    for power in (9, 7, 5, 3, 1):
        sign = 1.0 if power % 4 == 1 else -1.0
        poly = poly * y + sign / math.factorial(power)
    return x * poly


def body(
    start_hbm,
    stop_hbm,
    freq_hbm,
    traces_ref,
    kernel_ref,
    response_ref,
    table_ref,
    start_ref,
    stop_ref,
    freq_ref,
    tr_buf,
    kbuf,
    pown,
    pside,
    pbuf,
    fbuf,
    gbuf,
    part,
    pout,
    zbuf,
    rbuf,
    table_buf,
    local_sem,
    ks_sem,
    kr_sem,
    side_sem,
    fs_sem,
    gs_sem,
    gr_sem,
    zs_sem,
    zr_sem,
    rs_sem,
):
    rcv = lax.axis_index("rcv")
    frq = lax.axis_index("frq")
    plane = rcv // LINE
    line = rcv % LINE
    high = frq // 2
    core = frq % 2
    ring = high * LINE + line
    row = plane // 4
    col = plane % 4

    on_plane = []
    for across, down in PLANE_STEPS:
        peer = ((row + down) % 4) * 4 + (col + across) % 4
        on_plane.append((peer, (peer * LINE + line, high * 2 + 1)))
    on_ring = []
    for i in range(RING - 1):
        peer = i + (i + RING - ring) // RING
        on_ring.append((peer, (plane * LINE + peer % LINE, (peer // LINE) * 2 + 1)))
    opposite = (rcv, (1 - high) * 2 + 1)
    sibling = (rcv, high * 2 + 1 - core)

    barrier = pltpu.get_barrier_semaphore()

    def greet(device):
        pl.semaphore_signal(barrier, inc=1, device_id=device, device_id_type=MESH)

    @pl.when(core == 1)
    def _():
        for _, device in on_ring + on_plane:
            greet(device)
        greet(sibling)
        for peer, _ in on_plane:
            greet((peer * LINE + line, high * 2))

    @pl.when(core == 0)
    def _():
        greet(sibling)

    traces_copy = pltpu.make_async_copy(traces_ref, tr_buf, local_sem.at[0])
    traces_copy.start()
    index_copies = [
        pltpu.make_async_copy(source, target, local_sem.at[2 + i])
        for i, (source, target) in enumerate(
            ((freq_hbm, freq_ref), (start_hbm, start_ref), (stop_hbm, stop_ref))
        )
    ]
    for copy in index_copies:
        copy.start()
    for copy in index_copies:
        copy.wait()
    table = tables(freq_ref, frq * TIME).astype(jnp.bfloat16)
    table_buf[...] = table
    table_copy = pltpu.make_async_copy(table_buf, table_ref, local_sem.at[5])
    table_copy.start()

    sample = frq * TIME + iota((RCV, TIME), 1)
    start = column(start_ref, RCV, (RCV, TIME))
    stop = column(stop_ref, RCV, (RCV, TIME))
    window = jnp.where((sample >= start) & (sample < stop), 1.0, 0.0).astype(jnp.bfloat16)
    traces_copy.wait()
    tapered = (tr_buf[...] * window[None]).reshape(ROWS * RCV, TIME)
    sums = lax.dot_general(
        table, tapered, (((1,), (1,)), ((), ())), preferred_element_type=jnp.float32
    )
    for j in range(GROUPS):
        for half in range(2):
            piece = sums[j * FC : (j + 1) * FC, half * 256 : (half + 1) * 256]
            pown[j, half * FC : (half + 1) * FC] = piece

    def columns(peer):
        return kernel_ref.at[:, :, :, pl.ds(pl.multiple_of(peer * SRC, SRC), SRC)]

    def remote(source, target, send_sem, recv_sem, device):
        return pltpu.make_async_remote_copy(
            src_ref=source,
            dst_ref=target,
            send_sem=send_sem,
            recv_sem=recv_sem,
            device_id=device,
            device_id_type=MESH,
        )

    def kernel_copy(group, to, slot, device):
        return remote(
            columns(to), kbuf.at[group, :, :, slot], ks_sem.at[to], kr_sem.at[group, slot], device
        )

    side_copy = remote(pown, pside, side_sem.at[0], side_sem.at[1], sibling)
    response_copy = remote(rbuf, response_ref, rs_sem.at[0], rs_sem.at[1], sibling)

    @pl.when(core == 0)
    def _():
        pl.semaphore_wait(barrier, PLANE)
        side_copy.start()
        for peer, device in on_plane:
            kernel_copy(0, peer, plane, device).start()
        kernel_copy(0, plane, plane, sibling).start()
        side_copy.wait_send()
        for peer, device in on_plane:
            kernel_copy(0, peer, plane, device).wait_send()
        kernel_copy(0, plane, plane, sibling).wait_send()
        response_copy.wait_recv()

    @pl.when(core == 1)
    def _():
        own_copy = pltpu.make_async_copy(
            columns(plane), kbuf.at[1, :, :, plane], local_sem.at[1]
        )
        own_copy.start()

        side_copy.wait_recv()
        for j in range(GROUPS):
            pown[j] = pown[j] + pside[j]
        for c in range(2):
            pbuf[c] = pown[(1 - high) * 2 + c].astype(jnp.bfloat16)

        pl.semaphore_wait(barrier, PLANE + RING - 1)

        sums_copy = remote(pbuf, fbuf, fs_sem.at[0], fs_sem.at[1], opposite)
        sums_copy.start()
        for peer, device in on_plane:
            kernel_copy(1, peer, plane, device).start()

        spread = (FC, HALF, HALF * RCV)
        own_row = iota(spread, 2) // RCV == iota(spread, 1)
        pick = iota((RCV, HALF * RCV), 1) % RCV == iota((RCV, HALF * RCV), 0)
        pick = jnp.where(pick, 1.0, 0.0).astype(jnp.bfloat16)
        sums_copy.wait_recv()
        for c in range(2):
            total = pown[high * 2 + c] + fbuf[c].astype(jnp.float32)
            total = total * (1.0 / math.sqrt(PADDED_LENGTH))
            for half in range(2):
                wide = jnp.broadcast_to(total[half * FC : (half + 1) * FC][:, None, :], spread)
                wide = jnp.where(own_row, wide, 0.0).astype(jnp.bfloat16)
                spectra = lax.dot_general(
                    pick,
                    wide.reshape(FC * HALF, HALF * RCV),
                    (((1,), (1,)), ((), ())),
                    preferred_element_type=jnp.float32,
                )
                at = c * LANES + half * 128
                gbuf[plane, :, at : at + 128] = spectra.astype(jnp.bfloat16)

        def spectra_copy(to, slot, device):
            return remote(gbuf.at[plane], gbuf.at[slot], gs_sem.at[to], gr_sem.at[slot], device)

        for peer, device in on_plane:
            spectra_copy(peer, plane, device).start()

        own_copy.wait()
        kernel_copy(0, plane, plane, sibling).wait_recv()
        for peer, device in on_plane:
            kernel_copy(0, peer, peer, device).wait_recv()
            kernel_copy(1, peer, peer, device).wait_recv()
        for peer, device in on_plane:
            spectra_copy(peer, peer, device).wait_recv()

        for group in range(2):
            flipped = []
            for half in range(2):
                at = group * LANES + half * 128
                block = gbuf[:, :, at : at + 128].reshape(PLANE * RCV, 128)
                flipped.append(block.astype(jnp.float32).T)
            for pair in range(FREQS // 2):
                halves = []
                for f in (pair * 2, pair * 2 + 1):
                    at = f * 2 * HALF
                    real = [block[at : at + HALF] for block in flipped]
                    imag = [block[at + HALF : at + 2 * HALF] for block in flipped]
                    left = jnp.concatenate(real + imag, axis=0).astype(jnp.bfloat16)
                    right = jnp.concatenate(imag + [-block for block in real], axis=0)
                    right = right.astype(jnp.bfloat16)
                    halves.append(
                        jnp.dot(
                            left,
                            kbuf[group, 0, f].reshape(PLANE * RCV, SRC),
                            preferred_element_type=jnp.float32,
                        )
                        + jnp.dot(
                            right,
                            kbuf[group, 1, f].reshape(PLANE * RCV, SRC),
                            preferred_element_type=jnp.float32,
                        )
                    )
                turned = jnp.concatenate(halves, axis=0).T
                at = group * LANES + pair * 128
                part[:, at : at + 128] = turned
                pout[:, at : at + 128] = turned.astype(jnp.bfloat16)

        def source_rows(place):
            return pl.ds(pl.multiple_of((place % LINE) * RCV, RCV), RCV)

        def ring_copy(to, slot, device):
            return remote(
                pout.at[source_rows(to)], zbuf.at[slot], zs_sem.at[to], zr_sem.at[slot], device
            )

        for peer, device in on_ring:
            ring_copy(peer, ring, device).start()

        zbuf[ring] = jnp.zeros((RCV, 2 * LANES), jnp.bfloat16)
        near = part[source_rows(ring)]
        far = jnp.zeros((RCV, 2 * LANES), jnp.float32)

        for peer, device in on_plane:
            kernel_copy(1, peer, plane, device).wait_send()
            spectra_copy(peer, plane, device).wait_send()
        sums_copy.wait_send()
        for peer, device in on_ring:
            ring_copy(peer, peer, device).wait_recv()

        for i in range(LINE):
            near = near + zbuf[high * LINE + i].astype(jnp.float32)
            far = far + zbuf[(1 - high) * LINE + i].astype(jnp.float32)
        rbuf[high] = near.astype(jnp.bfloat16)
        rbuf[1 - high] = far.astype(jnp.bfloat16)

        own_response = pltpu.make_async_copy(rbuf, response_ref, local_sem.at[6])
        own_response.start()
        response_copy.start()
        for peer, device in on_ring:
            ring_copy(peer, ring, device).wait_send()
        own_response.wait()
        response_copy.wait_send()

    table_copy.wait()


def inverse(response_hbm, table_hbm, out_hbm, response, table, texp, lhs, result, in_sem, out_sem):
    copies = [
        pltpu.make_async_copy(table_hbm, table, in_sem.at[0]),
        pltpu.make_async_copy(response_hbm, response, in_sem.at[1]),
    ]
    for copy in copies:
        copy.start()
    own = iota((8, RCV, 128), 2) % 8 == iota((8, RCV, 128), 0)
    own = jnp.where(own, 1.0, 0.0).astype(jnp.bfloat16)
    slot = iota((RCV, 128), 1) // 8 % 4
    copies[0].wait()
    for m in range(2):
        for q in range(4):
            for i in range(4):
                row = (4 * m + i) * 4 + q
                at = m * 128 + 32 * q + 8 * i
                texp[at : at + 8] = jnp.broadcast_to(table[row : row + 1], (8, TIME))
    copies[1].wait()
    for m in range(2):
        tiles = []
        for i in range(4):
            tiles.append(response[m, :, i * 128 : (i + 1) * 128].astype(jnp.float32))
        for a in range(ROWS // 8):
            merged = tiles[a]
            for i in range(4):
                if i != a:
                    turned = pltpu.roll(tiles[i], 8 * (i - a) % 128, 1)
                    merged = jnp.where(slot == i, turned, merged)
            terms = merged.astype(jnp.bfloat16)[None] * own
            lhs[a * 128 : (a + 1) * 128, m * 128 : (m + 1) * 128] = terms.reshape(128, 128)
    pieces = []
    for n in range(TIME // PIECE):
        samples = slice(n * PIECE, (n + 1) * PIECE)
        traces_out = jnp.dot(lhs[...], texp[:, samples], preferred_element_type=jnp.float32)
        traces_out = traces_out * (1.0 / math.sqrt(BAND_FREQUENCIES))
        result[n] = traces_out.reshape(ROWS, RCV, PIECE)
        pieces.append(
            pltpu.make_async_copy(result.at[n], out_hbm.at[:, :, samples], out_sem.at[n])
        )
        pieces[-1].start()
    for piece in pieces:
        piece.wait()


def per_device(traces, taper_start, taper_stop, freq_index, kernel):
    hbm = pl.BlockSpec(memory_space=pltpu.HBM)
    dma = pltpu.SemaphoreType.DMA
    response, table = pl.pallas_call(
        body,
        out_shape=[
            jax.ShapeDtypeStruct((2, RCV, 2 * LANES), jnp.bfloat16),
            jax.ShapeDtypeStruct((2 * BAND_FREQUENCIES, TIME), jnp.bfloat16),
        ],
        in_specs=[hbm] * 5,
        out_specs=[hbm] * 2,
        scratch_shapes=[
            pltpu.SMEM((RCV,), jnp.int32),
            pltpu.SMEM((RCV,), jnp.int32),
            pltpu.SMEM((BAND_FREQUENCIES,), jnp.int32),
            pltpu.VMEM((ROWS, RCV, TIME), jnp.bfloat16),
            pltpu.VMEM((2, 2, FREQS, PLANE, RCV, SRC), jnp.bfloat16),
            pltpu.VMEM((GROUPS, 2 * FC, HALF * RCV), jnp.float32),
            pltpu.VMEM((GROUPS, 2 * FC, HALF * RCV), jnp.float32),
            pltpu.VMEM((2, 2 * FC, HALF * RCV), jnp.bfloat16),
            pltpu.VMEM((2, 2 * FC, HALF * RCV), jnp.bfloat16),
            pltpu.VMEM((PLANE, RCV, 2 * LANES), jnp.bfloat16),
            pltpu.VMEM((SRC, 2 * LANES), jnp.float32),
            pltpu.VMEM((SRC, 2 * LANES), jnp.bfloat16),
            pltpu.VMEM((RING, RCV, 2 * LANES), jnp.bfloat16),
            pltpu.VMEM((2, RCV, 2 * LANES), jnp.bfloat16),
            pltpu.VMEM((2 * BAND_FREQUENCIES, TIME), jnp.bfloat16),
            dma((7,)),
            dma((PLANE,)),
            dma((2, PLANE)),
            dma((2,)),
            dma((2,)),
            dma((PLANE,)),
            dma((PLANE,)),
            dma((RING,)),
            dma((RING,)),
            dma((2,)),
        ],
        compiler_params=pltpu.CompilerParams(
            collective_id=0, has_side_effects=True, vmem_limit_bytes=60 * 1024 * 1024
        ),
        cost_estimate=pl.CostEstimate(
            flops=2 * 40_000_000, bytes_accessed=1024 * 1024, transcendentals=0
        ),
    )(taper_start, taper_stop, freq_index, traces, kernel)
    return pl.pallas_call(
        inverse,
        out_shape=jax.ShapeDtypeStruct((ROWS, RCV, TIME), jnp.float32),
        in_specs=[hbm] * 2,
        out_specs=hbm,
        scratch_shapes=[
            pltpu.VMEM((2, RCV, 2 * LANES), jnp.bfloat16),
            pltpu.VMEM((2 * BAND_FREQUENCIES, TIME), jnp.bfloat16),
            pltpu.VMEM((256, TIME), jnp.bfloat16),
            pltpu.VMEM((ROWS * RCV, 256), jnp.bfloat16),
            pltpu.VMEM((TIME // PIECE, ROWS, RCV, PIECE), jnp.float32),
            dma((2,)),
            dma((TIME // PIECE,)),
        ],
        compiler_params=pltpu.CompilerParams(vmem_limit_bytes=60 * 1024 * 1024),
        cost_estimate=pl.CostEstimate(
            flops=2 * 8_400_000, bytes_accessed=1024 * 1024, transcendentals=0
        ),
    )(response, table)


def solution(mesh):
    in_specs = (P(None, "rcv", "frq"), P("rcv"), P("rcv"), P(), P(None, "frq", "rcv", None))
    out_specs = P(None, "rcv", "frq")
    return jax.shard_map(
        per_device, mesh=mesh, in_specs=in_specs, out_specs=out_specs, check_vma=False
    )
```

time: 43.3 us -> 39.8 us (0.919)
  Pallas kernels: 43 us -> 39.6 us
    pallas_call x1, Pallas kernels: 40.9 us -> 37.4 us  [per_device(): pl.pallas_call(body, out_shape=[jax.ShapeDtypeStruct((2, RCV, 2 * LANES),...]
where the time goes in v4:
time: 39.8 us; the launch traced here: 39.6 us
  Pallas kernels  39.6 us (99%)
    pallas_call x1, Pallas kernels, per_device(): pl.pallas_call(body, out_shape=[jax.ShapeDtypeStruct((2, RCV, 2 * LANES),...  37.4 us
    pallas_call x1, Pallas kernels, per_device(): pl.pallas_call(inverse, out_shape=jax.ShapeDtypeStruct((ROWS, RCV, TIME),...  2.17 us

profile of v4, /device:TPU:1, one launch (start us, length us, event | category | flops | bytes accessed | tf_op | source)
XLA Modules:
  0.0 39.6 jit_solution(15073703484299434595)
XLA Ops:
  0.0 37.4 %shard_map.55 = (bf16[2,16,512]{2,1,0:T(8,128)(2,1)}, bf16[32,512]{1,0:T(8,128)(2,1)}) custom-call(s32[16]{0:T(128)} %start_hbm.1, s32[16]{0:T(128)} %stop_hbm.1, s32[16]{0:T(128)} %freq_hbm.1, bf16[32,16,512]{2,1,0:T(8,128)(2,1)} %traces_ref.1, bf16[2,4,16,2048]{3,2,1,0:T(8,128)(2,1)} %kernel_ref.1), custom_call_target="tpu_custom_call" | custom-call | flops 80000000 | bytes 1048576 | tf_op jit(solution)/shard_map/pallas_call | solution.py:373
  37.5 2.2 %shard_map.56 = f32[32,16,512]{2,1,0:T(8,128)} custom-call(bf16[2,16,512]{2,1,0:T(8,128)(2,1)} %get-tuple-element.7.response_hbm, bf16[32,512]{1,0:T(8,128)(2,1)} %get-tuple-element.8.table_hbm), custom_call_target="tpu_custom_call" | custom-call | flops 16800000 | bytes 1048576 | tf_op jit(solution)/shard_map/pallas_call | solution.py:415

commit v5 on v4

--- a/solution.py
+++ b/solution.py
@@ -295,7 +295,6 @@
         for peer, device in on_ring:
             ring_copy(peer, ring, device).start()
 
-        zbuf[ring] = jnp.zeros((RCV, 2 * LANES), jnp.bfloat16)
         near = part[source_rows(ring)]
         far = jnp.zeros((RCV, 2 * LANES), jnp.float32)
 
@@ -303,12 +302,14 @@
             kernel_copy(1, peer, plane, device).wait_send()
             spectra_copy(peer, plane, device).wait_send()
         sums_copy.wait_send()
-        for peer, device in on_ring:
-            ring_copy(peer, peer, device).wait_recv()
-
-        for i in range(LINE):
-            near = near + zbuf[high * LINE + i].astype(jnp.float32)
-            far = far + zbuf[(1 - high) * LINE + i].astype(jnp.float32)
+        for step in range(1, LINE):
+            peer = high * LINE + (line + step) % LINE
+            ring_copy(peer, peer, opposite).wait_recv()
+            near = near + zbuf[peer].astype(jnp.float32)
+        for step in range(LINE):
+            peer = (1 - high) * LINE + (line + LINE - 1 - step) % LINE
+            ring_copy(peer, peer, opposite).wait_recv()
+            far = far + zbuf[peer].astype(jnp.float32)
         rbuf[high] = near.astype(jnp.bfloat16)
         rbuf[1 - high] = far.astype(jnp.bfloat16)
 
@@ -334,12 +335,15 @@
     own = jnp.where(own, 1.0, 0.0).astype(jnp.bfloat16)
     slot = iota((RCV, 128), 1) // 8 % 4
     copies[0].wait()
+    rows = table[...].astype(jnp.float32)
     for m in range(2):
         for q in range(4):
+            block = []
             for i in range(4):
                 row = (4 * m + i) * 4 + q
-                at = m * 128 + 32 * q + 8 * i
-                texp[at : at + 8] = jnp.broadcast_to(table[row : row + 1], (8, TIME))
+                block.append(jnp.broadcast_to(rows[row : row + 1], (8, TIME)))
+            at = m * 128 + 32 * q
+            texp[at : at + 32] = jnp.concatenate(block, axis=0).astype(jnp.bfloat16)
     copies[1].wait()
     for m in range(2):
         tiles = []

time: 39.8 us -> 39.8 us (level)
  no operation moved by 1% of the time
where the time goes in v5:
time: 39.8 us; the launch traced here: 39.6 us
  Pallas kernels  39.5 us (99%)
    pallas_call x1, Pallas kernels, per_device(): pl.pallas_call(body, out_shape=[jax.ShapeDtypeStruct((2, RCV, 2 * LANES),...  37.4 us
    pallas_call x1, Pallas kernels, per_device(): pl.pallas_call(inverse, out_shape=jax.ShapeDtypeStruct((ROWS, RCV, TIME),...  2.14 us

profile of v5, /device:TPU:1, one launch (start us, length us, event | category | flops | bytes accessed | tf_op | source)
XLA Modules:
  0.0 39.6 jit_solution(7585816832378457311)
XLA Ops:
  0.0 37.4 %shard_map.55 = (bf16[2,16,512]{2,1,0:T(8,128)(2,1)}, bf16[32,512]{1,0:T(8,128)(2,1)}) custom-call(s32[16]{0:T(128)} %start_hbm.1, s32[16]{0:T(128)} %stop_hbm.1, s32[16]{0:T(128)} %freq_hbm.1, bf16[32,16,512]{2,1,0:T(8,128)(2,1)} %traces_ref.1, bf16[2,4,16,2048]{3,2,1,0:T(8,128)(2,1)} %kernel_ref.1), custom_call_target="tpu_custom_call" | custom-call | flops 80000000 | bytes 1048576 | tf_op jit(solution)/shard_map/pallas_call | solution.py:377
  37.4 2.1 %shard_map.56 = f32[32,16,512]{2,1,0:T(8,128)} custom-call(bf16[2,16,512]{2,1,0:T(8,128)(2,1)} %get-tuple-element.7.response_hbm, bf16[32,512]{1,0:T(8,128)(2,1)} %get-tuple-element.8.table_hbm), custom_call_target="tpu_custom_call" | custom-call | flops 16800000 | bytes 1048576 | tf_op jit(solution)/shard_map/pallas_call | solution.py:419

commit v6 on v5

--- a/solution.py
+++ b/solution.py
@@ -34,13 +34,13 @@
     return lax.broadcasted_iota(jnp.int32, shape, axis)
 
 
-def column(ref, count, shape):
+def column(ref, count, shape, first=0):
     rows = shape[0]
     each = rows // count
     row = iota(shape, 0) // each
-    out = jnp.full(shape, ref[0], jnp.int32)
+    out = jnp.full(shape, ref[first], jnp.int32)
     for i in range(1, count):
-        out = jnp.where(row == i, ref[i], out)
+        out = jnp.where(row == i, ref[first + i], out)
     return out
 
 
@@ -62,16 +62,12 @@
 
 
 def body(
-    start_hbm,
-    stop_hbm,
-    freq_hbm,
+    index_hbm,
     traces_ref,
     kernel_ref,
     response_ref,
     table_ref,
-    start_ref,
-    stop_ref,
-    freq_ref,
+    index_ref,
     tr_buf,
     kbuf,
     pown,
@@ -82,8 +78,6 @@
     part,
     pout,
     zbuf,
-    rbuf,
-    table_buf,
     local_sem,
     ks_sem,
     kr_sem,
@@ -135,24 +129,15 @@
 
     traces_copy = pltpu.make_async_copy(traces_ref, tr_buf, local_sem.at[0])
     traces_copy.start()
-    index_copies = [
-        pltpu.make_async_copy(source, target, local_sem.at[2 + i])
-        for i, (source, target) in enumerate(
-            ((freq_hbm, freq_ref), (start_hbm, start_ref), (stop_hbm, stop_ref))
-        )
-    ]
-    for copy in index_copies:
-        copy.start()
-    for copy in index_copies:
-        copy.wait()
-    table = tables(freq_ref, frq * TIME).astype(jnp.bfloat16)
-    table_buf[...] = table
-    table_copy = pltpu.make_async_copy(table_buf, table_ref, local_sem.at[5])
-    table_copy.start()
+    index_copy = pltpu.make_async_copy(index_hbm, index_ref, local_sem.at[2])
+    index_copy.start()
+    index_copy.wait()
+    table = tables(index_ref, frq * TIME).astype(jnp.bfloat16)
+    table_ref[...] = table
 
     sample = frq * TIME + iota((RCV, TIME), 1)
-    start = column(start_ref, RCV, (RCV, TIME))
-    stop = column(stop_ref, RCV, (RCV, TIME))
+    start = column(index_ref, RCV, (RCV, TIME), BAND_FREQUENCIES)
+    stop = column(index_ref, RCV, (RCV, TIME), BAND_FREQUENCIES + RCV)
     window = jnp.where((sample >= start) & (sample < stop), 1.0, 0.0).astype(jnp.bfloat16)
     traces_copy.wait()
     tapered = (tr_buf[...] * window[None]).reshape(ROWS * RCV, TIME)
@@ -183,7 +168,7 @@
         )
 
     side_copy = remote(pown, pside, side_sem.at[0], side_sem.at[1], sibling)
-    response_copy = remote(rbuf, response_ref, rs_sem.at[0], rs_sem.at[1], sibling)
+    response_copy = remote(response_ref, response_ref, rs_sem.at[0], rs_sem.at[1], sibling)
 
     @pl.when(core == 0)
     def _():
@@ -310,31 +295,19 @@
             peer = (1 - high) * LINE + (line + LINE - 1 - step) % LINE
             ring_copy(peer, peer, opposite).wait_recv()
             far = far + zbuf[peer].astype(jnp.float32)
-        rbuf[high] = near.astype(jnp.bfloat16)
-        rbuf[1 - high] = far.astype(jnp.bfloat16)
-
-        own_response = pltpu.make_async_copy(rbuf, response_ref, local_sem.at[6])
-        own_response.start()
+        response_ref[high] = near.astype(jnp.bfloat16)
+        response_ref[1 - high] = far.astype(jnp.bfloat16)
+
         response_copy.start()
         for peer, device in on_ring:
             ring_copy(peer, ring, device).wait_send()
-        own_response.wait()
         response_copy.wait_send()
 
-    table_copy.wait()
-
-
-def inverse(response_hbm, table_hbm, out_hbm, response, table, texp, lhs, result, in_sem, out_sem):
-    copies = [
-        pltpu.make_async_copy(table_hbm, table, in_sem.at[0]),
-        pltpu.make_async_copy(response_hbm, response, in_sem.at[1]),
-    ]
-    for copy in copies:
-        copy.start()
+
+def inverse(response, table, out_hbm, texp, lhs, result, out_sem):
     own = iota((8, RCV, 128), 2) % 8 == iota((8, RCV, 128), 0)
     own = jnp.where(own, 1.0, 0.0).astype(jnp.bfloat16)
     slot = iota((RCV, 128), 1) // 8 % 4
-    copies[0].wait()
     rows = table[...].astype(jnp.float32)
     for m in range(2):
         for q in range(4):
@@ -344,7 +317,6 @@
                 block.append(jnp.broadcast_to(rows[row : row + 1], (8, TIME)))
             at = m * 128 + 32 * q
             texp[at : at + 32] = jnp.concatenate(block, axis=0).astype(jnp.bfloat16)
-    copies[1].wait()
     for m in range(2):
         tiles = []
         for i in range(4):
@@ -373,6 +345,7 @@
 
 def per_device(traces, taper_start, taper_stop, freq_index, kernel):
     hbm = pl.BlockSpec(memory_space=pltpu.HBM)
+    vmem = pl.BlockSpec(memory_space=pltpu.VMEM)
     dma = pltpu.SemaphoreType.DMA
     response, table = pl.pallas_call(
         body,
@@ -380,12 +353,10 @@
             jax.ShapeDtypeStruct((2, RCV, 2 * LANES), jnp.bfloat16),
             jax.ShapeDtypeStruct((2 * BAND_FREQUENCIES, TIME), jnp.bfloat16),
         ],
-        in_specs=[hbm] * 5,
-        out_specs=[hbm] * 2,
+        in_specs=[hbm] * 3,
+        out_specs=[vmem] * 2,
         scratch_shapes=[
-            pltpu.SMEM((RCV,), jnp.int32),
-            pltpu.SMEM((RCV,), jnp.int32),
-            pltpu.SMEM((BAND_FREQUENCIES,), jnp.int32),
+            pltpu.SMEM((BAND_FREQUENCIES + 2 * RCV,), jnp.int32),
             pltpu.VMEM((ROWS, RCV, TIME), jnp.bfloat16),
             pltpu.VMEM((2, 2, FREQS, PLANE, RCV, SRC), jnp.bfloat16),
             pltpu.VMEM((GROUPS, 2 * FC, HALF * RCV), jnp.float32),
@@ -396,9 +367,7 @@
             pltpu.VMEM((SRC, 2 * LANES), jnp.float32),
             pltpu.VMEM((SRC, 2 * LANES), jnp.bfloat16),
             pltpu.VMEM((RING, RCV, 2 * LANES), jnp.bfloat16),
-            pltpu.VMEM((2, RCV, 2 * LANES), jnp.bfloat16),
-            pltpu.VMEM((2 * BAND_FREQUENCIES, TIME), jnp.bfloat16),
-            dma((7,)),
+            dma((3,)),
             dma((PLANE,)),
             dma((2, PLANE)),
             dma((2,)),
@@ -410,27 +379,24 @@
             dma((2,)),
         ],
         compiler_params=pltpu.CompilerParams(
-            collective_id=0, has_side_effects=True, vmem_limit_bytes=60 * 1024 * 1024
+            collective_id=0, has_side_effects=True, vmem_limit_bytes=54784 * 1024
         ),
         cost_estimate=pl.CostEstimate(
             flops=2 * 40_000_000, bytes_accessed=1024 * 1024, transcendentals=0
         ),
-    )(taper_start, taper_stop, freq_index, traces, kernel)
+    )(jnp.concatenate([freq_index, taper_start, taper_stop]), traces, kernel)
     return pl.pallas_call(
         inverse,
         out_shape=jax.ShapeDtypeStruct((ROWS, RCV, TIME), jnp.float32),
-        in_specs=[hbm] * 2,
+        in_specs=[vmem] * 2,
         out_specs=hbm,
         scratch_shapes=[
-            pltpu.VMEM((2, RCV, 2 * LANES), jnp.bfloat16),
-            pltpu.VMEM((2 * BAND_FREQUENCIES, TIME), jnp.bfloat16),
             pltpu.VMEM((256, TIME), jnp.bfloat16),
             pltpu.VMEM((ROWS * RCV, 256), jnp.bfloat16),
             pltpu.VMEM((TIME // PIECE, ROWS, RCV, PIECE), jnp.float32),
-            dma((2,)),
             dma((TIME // PIECE,)),
         ],
-        compiler_params=pltpu.CompilerParams(vmem_limit_bytes=60 * 1024 * 1024),
+        compiler_params=pltpu.CompilerParams(vmem_limit_bytes=16 * 1024 * 1024),
         cost_estimate=pl.CostEstimate(
             flops=2 * 8_400_000, bytes_accessed=1024 * 1024, transcendentals=0
         ),

time: 39.8 us -> 39.5 us (level)
  Pallas kernels: 39.5 us -> 38.6 us
  other arithmetic: 0 us -> 0.76 us
    pallas_call x1, Pallas kernels: 2.14 us -> 1.34 us  [per_device(): pl.pallas_call(inverse, out_shape=jax.ShapeDtypeStruct((ROWS, RCV, TIME),...]
    concatenate x0 -> x1, other arithmetic: none -> 0.76 us  [per_device(): jnp.concatenate([freq_index, taper_start, taper_stop])]
where the time goes in v6:
time: 39.5 us; the launch traced here: 39.3 us
  Pallas kernels  38.6 us (98%)
  other arithmetic  0.76 us (2%)
    pallas_call x1, Pallas kernels, per_device(): pl.pallas_call(body, out_shape=[jax.ShapeDtypeStruct((2, RCV, 2 * LANES),...  37.2 us
    pallas_call x1, Pallas kernels, per_device(): pl.pallas_call(inverse, out_shape=jax.ShapeDtypeStruct((ROWS, RCV, TIME),...  1.34 us

profile of v6, /device:TPU:1, one launch (start us, length us, event | category | flops | bytes accessed | tf_op | source)
XLA Modules:
  0.0 39.3 jit_solution(8410314891587923879)
XLA Ops:
  0.0 0.8 %pad_add_fusion.index_hbm = s32[48]{0:T(128)S(1)} fusion(s32[16]{0:T(128)} %param.7, s32[16]{0:T(128)} %param.6, s32[16]{0:T(128)} %param.8), kind=kLoop, calls=%fused_computation | loop fusion | flops 96 | bytes 384 | tf_op jit(solution)/shard_map/concatenate | solution.py:387
  0.8 37.2 %shard_map.55 = (bf16[2,16,512]{2,1,0:T(8,128)(2,1)S(1)}, bf16[32,512]{1,0:T(8,128)(2,1)S(1)}) custom-call(s32[48]{0:T(128)S(1)} %pad_add_fusion.index_hbm, bf16[32,16,512]{2,1,0:T(8,128)(2,1)} %traces_ref.1, bf16[2,4,16,2048]{3,2,1,0:T(8,128)(2,1)} %kernel_ref.1), custom_call_target="tpu_custom_call" | custom-call | flops 80000000 | bytes 1048576 | tf_op jit(solution)/shard_map/pallas_call | solution.py:350
  38.0 1.3 %shard_map.56 = f32[32,16,512]{2,1,0:T(8,128)} custom-call(bf16[2,16,512]{2,1,0:T(8,128)(2,1)S(1)} %get-tuple-element.7.response, bf16[32,512]{1,0:T(8,128)(2,1)S(1)} %get-tuple-element.8.table), custom_call_target="tpu_custom_call" | custom-call | flops 16800000 | bytes 1048576 | tf_op jit(solution)/shard_map/pallas_call | solution.py:388

commit v7 on v6

--- a/solution.py
+++ b/solution.py
@@ -226,8 +226,9 @@
         def spectra_copy(to, slot, device):
             return remote(gbuf.at[plane], gbuf.at[slot], gs_sem.at[to], gr_sem.at[slot], device)
 
-        for peer, device in on_plane:
-            spectra_copy(peer, plane, device).start()
+        for i in range(PLANE - 1):
+            peer = i + (i + PLANE - plane) // PLANE
+            spectra_copy(peer, plane, (peer * LINE + line, high * 2 + 1)).start()
 
         own_copy.wait()
         kernel_copy(0, plane, plane, sibling).wait_recv()
@@ -287,6 +288,8 @@
             kernel_copy(1, peer, plane, device).wait_send()
             spectra_copy(peer, plane, device).wait_send()
         sums_copy.wait_send()
+        for peer, device in on_ring:
+            ring_copy(peer, ring, device).wait_send()
         for step in range(1, LINE):
             peer = high * LINE + (line + step) % LINE
             ring_copy(peer, peer, opposite).wait_recv()
@@ -299,8 +302,6 @@
         response_ref[1 - high] = far.astype(jnp.bfloat16)
 
         response_copy.start()
-        for peer, device in on_ring:
-            ring_copy(peer, ring, device).wait_send()
         response_copy.wait_send()
 
 

time: 39.5 us -> 39.4 us (level)
  no operation moved by 1% of the time
where the time goes in v7:
time: 39.4 us; the launch traced here: 39.2 us
  Pallas kernels  38.4 us (97%)
  other arithmetic  0.76 us (2%)
    pallas_call x1, Pallas kernels, per_device(): pl.pallas_call(body, out_shape=[jax.ShapeDtypeStruct((2, RCV, 2 * LANES),...  37.1 us
    pallas_call x1, Pallas kernels, per_device(): pl.pallas_call(inverse, out_shape=jax.ShapeDtypeStruct((ROWS, RCV, TIME),...  1.34 us

profile of v7, /device:TPU:1, one launch (start us, length us, event | category | flops | bytes accessed | tf_op | source)
XLA Modules:
  0.0 39.2 jit_solution(17091437077588653494)
XLA Ops:
  0.0 0.8 %pad_add_fusion.index_hbm = s32[48]{0:T(128)S(1)} fusion(s32[16]{0:T(128)} %param.7, s32[16]{0:T(128)} %param.6, s32[16]{0:T(128)} %param.8), kind=kLoop, calls=%fused_computation | loop fusion | flops 96 | bytes 384 | tf_op jit(solution)/shard_map/concatenate | solution.py:388
  0.8 37.1 %shard_map.55 = (bf16[2,16,512]{2,1,0:T(8,128)(2,1)S(1)}, bf16[32,512]{1,0:T(8,128)(2,1)S(1)}) custom-call(s32[48]{0:T(128)S(1)} %pad_add_fusion.index_hbm, bf16[32,16,512]{2,1,0:T(8,128)(2,1)} %traces_ref.1, bf16[2,4,16,2048]{3,2,1,0:T(8,128)(2,1)} %kernel_ref.1), custom_call_target="tpu_custom_call" | custom-call | flops 80000000 | bytes 1048576 | tf_op jit(solution)/shard_map/pallas_call | solution.py:351
  37.9 1.3 %shard_map.56 = f32[32,16,512]{2,1,0:T(8,128)} custom-call(bf16[2,16,512]{2,1,0:T(8,128)(2,1)S(1)} %get-tuple-element.7.response, bf16[32,512]{1,0:T(8,128)(2,1)S(1)} %get-tuple-element.8.table), custom_call_target="tpu_custom_call" | custom-call | flops 16800000 | bytes 1048576 | tf_op jit(solution)/shard_map/pallas_call | solution.py:389
